TPU v7x, 256 devices: a whole 4x4x8 slice. The times are simulated.
256 devices in a mesh: section: 2 (over y_hi), dp: 16 (over y_lo, x, core), mp: 8 (over z).
Axes of the slice: x: 4, y: 4 (y_hi: 2, y_lo: 2; y = y_hi * 2 + y_lo), z: 8, core: 2. Of those that a mesh axis runs over, the one named last changes fastest.
Arguments:
- activations: bfloat16 [2, 1024, 4096], P(None, 'dp'), may hold values from -6 to 6
- cotangent: bfloat16 [2, 1024, 4096], P(None, 'dp'), may hold values from -6 to 6
- norm_gain: float32 [2, 4096], P('section'), may hold values from 0.1 to 1.9
- w_up: bfloat16 [2, 4096, 8192], P('section', 'dp', 'mp'), may hold values from -0.09375 to 0.09375
- w_down: bfloat16 [2, 4096, 8192], P('section', 'dp', 'mp'), may hold values from -0.0625 to 0.0625
- gram_left: float32 [2, 128, 512, 512], P('section', ('dp', 'mp')), as said below
- gram_right: float32 [2, 128, 512, 512], P('section', ('dp', 'mp')), as said below
- root_left: bfloat16 [2, 128, 512, 512], P('section', ('dp', 'mp'))
- root_right: bfloat16 [2, 128, 512, 512], P('section', ('dp', 'mp'))
- owner_slot: int32 [2, 16, 8], replicated, may hold values from 0 to 127, as said below
- eighth: int32 [2, 16, 8], replicated, may hold values from 0 to 7, as said below
- refresh_phase: int32 [1], replicated, may hold values from 0 to 999999
Outputs:
- new_gram_left: float32 [2, 128, 512, 512], P('section', ('dp', 'mp'))
- new_gram_right: float32 [2, 128, 512, 512], P('section', ('dp', 'mp'))
- new_root_left: bfloat16 [2, 128, 512, 512], P('section', ('dp', 'mp'))
- new_root_right: bfloat16 [2, 128, 512, 512], P('section', ('dp', 'mp'))
- update_blocks: bfloat16 [2, 128, 512, 512], P('section', ('dp', 'mp'))
Inputs may be any that keep to these rules, and one draw needn't show every extreme that they name: `owner_slot`: for each section, a permutation of the 128 slots; the block of flat index f = i * 8 + j goes to a slot t with (t) % (8) == f // 16. `eighth`: in each section and each run of 16 consecutive flat block indices, every value is taken by exactly 2 blocks. `gram_left`: symmetric positive definite. `gram_right`: symmetric positive definite.
All inputs are finite; a program needn't handle non-finite values.
Results may differ from a plain program's by a relative error of at most 0.025.
Values may be sent and summed in bfloat16 or wider, within the bound.
No kernel may reach another device: no remote copies, remote signals or barrier semaphores. Data moves between devices by JAX's collectives and lax.ppermute only.
A program may use at most 128 MiB of HBM per device.

v0:
```python
import math

import jax
import jax.numpy as jnp
from jax import lax
from jax.sharding import PartitionSpec as P

BLK = 512
ITERS = 2


norm_epsilon = 1e-05
decay_rate = 0.9
ridge_shift = 0.001
highest = lax.Precision.HIGHEST


def passed_along(block, axis, distance):
    devices = range(lax.axis_size(axis))
    route = [(i - distance, i) for i in devices if i - distance in devices]
    return lax.ppermute(block, axis, route)


def normalize_values(values, gain_row):
    inverse_rms = lax.rsqrt(jnp.mean(values * values, axis=-1, keepdims=True) + norm_epsilon)
    return values * inverse_rms * gain_row


def silu_slope(pre_act):
    sigmoid_values = jax.nn.sigmoid(pre_act)
    return sigmoid_values * (1.0 + pre_act * (1.0 - sigmoid_values))


def inverse_root(matrix):
    matrix_order = matrix.shape[-1]
    identity = jnp.eye(matrix_order, dtype=jnp.float32)
    shifted = matrix + ridge_shift * identity
    factor = 2.5 / jnp.sqrt(jnp.sum(shifted * shifted))
    iterate = jnp.power(factor, 0.25) * identity
    moment = factor * shifted
    for sweep_no in range(ITERS):
        step_mat = 1.25 * identity - 0.25 * moment
        square = jnp.dot(step_mat, step_mat, precision=highest)
        fourth = jnp.dot(square, square, precision=highest)
        moment = jnp.dot(fourth, moment, precision=highest)
        iterate = jnp.dot(iterate, step_mat, precision=highest)
    return iterate


def forward_layer(inputs, gain_row, up_rows, down_rows):
    values = inputs.astype(jnp.float32)
    normed = normalize_values(values, gain_row).astype(jnp.bfloat16)
    pre_act = jnp.dot(normed, up_rows, preferred_element_type=jnp.float32)
    hidden = jax.nn.silu(pre_act).astype(jnp.bfloat16)
    partial_value = lax.dot_general(
        hidden, down_rows, (((1,), (1,)), ((), ())), preferred_element_type=jnp.float32
    )
    branch = lax.psum(partial_value.astype(jnp.bfloat16), "mp").astype(jnp.float32)
    output = (values + branch).astype(jnp.bfloat16)
    return (output, pre_act, hidden)


def backward_layer(grad_output, inputs, pre_act, gain_row, up_rows, down_rows):
    grad_hidden = jnp.dot(grad_output, down_rows, preferred_element_type=jnp.float32)
    grad_pre = (grad_hidden * silu_slope(pre_act)).astype(jnp.bfloat16)
    partial_value = lax.dot_general(
        grad_pre, up_rows, (((1,), (1,)), ((), ())), preferred_element_type=jnp.float32
    )
    grad_normed = lax.psum(partial_value.astype(jnp.bfloat16), "mp").astype(jnp.float32)
    values = inputs.astype(jnp.float32)
    unused, pullback = jax.vjp(lambda values_in: normalize_values(values_in, gain_row), values)
    grad_values = pullback(grad_normed)[0]
    return (grad_output.astype(jnp.float32) + grad_values).astype(jnp.bfloat16)


def store_row(stack, entry, slot_index, is_valid):
    return jnp.where(is_valid, lax.dynamic_update_index_in_dim(stack, entry, slot_index, 0), stack)


def on_device(
    activations,
    cotangent,
    norm_gain,
    w_up,
    w_down,
    gram_left,
    gram_right,
    root_left,
    root_right,
    owner_slot,
    eighth,
    refresh_phase,
):
    section_no = lax.axis_index("section")
    dp_no = lax.axis_index("dp")
    mp_no = lax.axis_index("mp")
    section_total = lax.axis_size("section")
    dp_count = lax.axis_size("dp")
    mp_count = lax.axis_size("mp")
    micro_count, row_count, model_width = activations.shape
    gain_row = norm_gain[0]
    up_full, down_full = (
        lax.all_gather(w_up[0], "dp", axis=0, tiled=True),
        lax.all_gather(w_down[0], "dp", axis=0, tiled=True),
    )
    shard_ff = up_full.shape[1]
    tick_total = micro_count + section_total - 1
    inputs_all = jnp.zeros((micro_count, row_count, model_width), jnp.bfloat16)
    pre_all = jnp.zeros((micro_count, row_count, shard_ff), jnp.float32)
    hidden_all = jnp.zeros((micro_count, row_count, shard_ff), jnp.bfloat16)
    received = jnp.zeros((row_count, model_width), jnp.bfloat16)
    is_first = section_no == 0
    for tick_no in range(tick_total):
        batch_no = tick_no - section_no
        is_valid = (batch_no >= 0) & (batch_no < micro_count)
        slot_index = jnp.clip(batch_no, 0, micro_count - 1)
        inputs = jnp.where(is_first, activations[min(tick_no, micro_count - 1)], received)
        output, pre_act, hidden = forward_layer(inputs, gain_row, up_full, down_full)
        inputs_all = store_row(inputs_all, inputs, slot_index, is_valid)
        pre_all = store_row(pre_all, pre_act, slot_index, is_valid)
        hidden_all = store_row(hidden_all, hidden, slot_index, is_valid)
        if tick_no < tick_total - 1:
            received = passed_along(output, "section", 1)
    grad_all = jnp.zeros((micro_count, row_count, model_width), jnp.bfloat16)
    received = jnp.zeros((row_count, model_width), jnp.bfloat16)
    is_last = section_no == section_total - 1
    for tick_no in range(tick_total):
        batch_no = tick_no - (section_total - 1 - section_no)
        is_valid = (batch_no >= 0) & (batch_no < micro_count)
        slot_index = jnp.clip(batch_no, 0, micro_count - 1)
        grad_output = jnp.where(is_last, cotangent[min(tick_no, micro_count - 1)], received)
        inputs = lax.dynamic_index_in_dim(inputs_all, slot_index, 0, keepdims=False)
        pre_act = lax.dynamic_index_in_dim(pre_all, slot_index, 0, keepdims=False)
        grad_all = store_row(grad_all, grad_output, slot_index, is_valid)
        grad_input = backward_layer(grad_output, inputs, pre_act, gain_row, up_full, down_full)
        if tick_no < tick_total - 1:
            received = passed_along(grad_input, "section", -1)
    token_count = micro_count * row_count
    block_rows = shard_ff // BLK
    block_cols = model_width // BLK
    group_size = block_rows * block_cols
    per_dev = group_size // dp_count
    hidden_flat = hidden_all.reshape(token_count, block_rows, BLK)
    grad_flat = grad_all.reshape(token_count, block_cols, BLK)
    section_owner = lax.dynamic_index_in_dim(owner_slot, section_no, 0, keepdims=False)
    local_owner = lax.dynamic_slice_in_dim(
        section_owner, mp_no * block_rows, block_rows, 0
    ).reshape(-1)
    local_slot = local_owner // (mp_count * per_dev) * per_dev + local_owner % per_dev
    block_of_slot = jnp.argsort(local_slot)
    row_of_slot = block_of_slot // block_cols
    col_of_slot = block_of_slot % block_cols
    hidden_slots = jnp.take(hidden_flat, row_of_slot, axis=1)
    grad_slots = jnp.take(grad_flat, col_of_slot, axis=1)
    hidden_recv, grad_recv = (
        lax.all_to_all(hidden_slots, "dp", split_axis=1, concat_axis=0, tiled=True),
        lax.all_to_all(grad_slots, "dp", split_axis=1, concat_axis=0, tiled=True),
    )
    hidden_in = hidden_recv.reshape(dp_count, token_count, per_dev, BLK)
    grad_in = grad_recv.reshape(dp_count, token_count, per_dev, BLK)
    products = jnp.einsum("snbk,snbl->sbkl", hidden_in, grad_in, preferred_element_type=jnp.float32)
    rounded = lax.optimization_barrier(products.astype(jnp.bfloat16)).astype(jnp.float32)
    summed = jnp.sum(rounded, axis=0)
    scaled = summed * (1.0 / math.sqrt(token_count * dp_count))
    left_new = (
        decay_rate * gram_left[0]
        + jnp.einsum("sij,skj->sik", scaled, scaled, precision=highest) / BLK
    )
    right_new = (
        decay_rate * gram_right[0]
        + jnp.einsum("sji,sjk->sik", scaled, scaled, precision=highest) / BLK
    )
    phase_now = refresh_phase[0] % 8
    section_eighth = lax.dynamic_index_in_dim(eighth, section_no, 0, keepdims=False)
    local_eighth = lax.dynamic_slice_in_dim(
        section_eighth, mp_no * block_rows, block_rows, 0
    ).reshape(-1)
    is_due = jnp.take(local_eighth, block_of_slot) == phase_now
    my_due = lax.dynamic_slice_in_dim(is_due, dp_no * per_dev, per_dev)

    def refresh_slot(operands):
        return lax.cond(
            operands[0],
            lambda ops: (
                inverse_root(ops[1]).astype(jnp.bfloat16),
                inverse_root(ops[2]).astype(jnp.bfloat16),
            ),
            lambda ops: (ops[3], ops[4]),
            operands,
        )

    roots_l, roots_r = lax.map(
        refresh_slot, (my_due, left_new, right_new, root_left[0], root_right[0])
    )
    grad_low = scaled.astype(jnp.bfloat16)
    inner_product = jnp.einsum(
        "sij,sjk->sik", grad_low, roots_r, preferred_element_type=jnp.float32
    ).astype(jnp.bfloat16)
    update = jnp.einsum(
        "sij,sjk->sik", roots_l, inner_product, preferred_element_type=jnp.float32
    ).astype(jnp.bfloat16)
    return (left_new[None], right_new[None], roots_l[None], roots_r[None], update[None])


def solution(mesh):
    return jax.shard_map(
        on_device,
        mesh=mesh,
        in_specs=(
            P(None, "dp", None),
            P(None, "dp", None),
            P("section", None),
            P("section", "dp", "mp"),
            P("section", "dp", "mp"),
            P("section", ("dp", "mp"), None, None),
            P("section", ("dp", "mp"), None, None),
            P("section", ("dp", "mp"), None, None),
            P("section", ("dp", "mp"), None, None),
            P(),
            P(),
            P(),
        ),
        out_specs=(
            P("section", ("dp", "mp"), None, None),
            P("section", ("dp", "mp"), None, None),
            P("section", ("dp", "mp"), None, None),
            P("section", ("dp", "mp"), None, None),
            P("section", ("dp", "mp"), None, None),
        ),
        check_vma=False,
    )
```

profile of v0, /device:TPU:10, one launch (start us, length us, event | category | flops | bytes accessed | tf_op | source)
XLA Modules:
  0.0 616.6 jit_solution(3433729664211271295)
XLA Ops:
  7.2 1.9 copy.58
  9.1 1.9 copy.59
  13.1 55.5 %all-gather.5.cloned.1.call-done = bf16[1,4096,1024]{2,1,0:T(8,128)(2,1)} async-done(((bf16[1,256,1024]{2,1,0:T(8,128)(2,1)}), bf16[1,4096,1024]{2,1,0:T(8,128)(2,1)}) %all-gather.5.cloned.1.call-update) | async-done | bytes 8388624 | tf_op jit(solution)/shard_map/all_gather | solution.py:103
  68.7 5.2 bitcast_dynamic-update-slice_fusion
  73.9 52.1 %all-gather.7.cloned.1.call-done = bf16[1,4096,1024]{2,1,0:T(8,128)(2,1)} async-done(((bf16[1,256,1024]{2,1,0:T(8,128)(2,1)}), bf16[1,4096,1024]{2,1,0:T(8,128)(2,1)}) %all-gather.7.cloned.1.call-update) | async-done | bytes 8388624 | tf_op jit(solution)/shard_map/all_gather | solution.py:104
  126.1 6.8 %fusion.72 = bf16[64,4096]{1,0:T(8,128)(2,1)} fusion(bf16[1,4096,1024]{2,1,0:T(8,128)(2,1)} %all-gather.7.cloned.1.call-done, f32[64,1024]{1,0:T(8,128)S(1)} %get-tuple-element.85), kind=kOutput, calls=%fused_computation.86 | convolution fusion | flops 537460736 | bytes 9175040 | tf_op jit(solution)/shard_map/dot_general | solution.py:55
  133.0 74.4 %all-reduce.5.cloned.1.call-done = bf16[64,4096]{1,0:T(8,128)(2,1)} async-done(((bf16[64,4096]{1,0:T(8,128)(2,1)}), bf16[64,4096]{1,0:T(8,128)(2,1)}) %all-reduce.5.cloned.1.call-update) | async-done | bytes 524304 | tf_op jit(solution)/shard_map/psum | solution.py:58
  208.6 4.1 collective-permute-start
  212.9 6.4 %collective-permute-done = bf16[64,4096]{1,0:T(8,128)(2,1)S(1)} collective-permute-done((bf16[64,4096]{1,0:T(8,128)(2,1)S(1)}, bf16[64,4096]{1,0:T(8,128)(2,1)S(1)}, u32[]{:S(2)}, u32[]{:S(2)}) %collective-permute-start) | collective-permute-done | bytes 524320 | tf_op jit(solution)/shard_map/ppermute | solution.py:21
  219.8 5.2 fusion.153
  225.7 3.5 fusion.75
  231.6 71.7 %all-reduce.7.cloned.1.call-done = bf16[64,4096]{1,0:T(8,128)(2,1)} async-done(((bf16[64,4096]{1,0:T(8,128)(2,1)}), bf16[64,4096]{1,0:T(8,128)(2,1)}) %all-reduce.7.cloned.1.call-update) | async-done | bytes 524304 | tf_op jit(solution)/shard_map/psum | solution.py:58
  304.4 4.6 collective-permute-start.1
  310.3 4.8 collective-permute-done.1
  315.6 5.9 fusion.152
  321.5 10.8 %fusion.66 = bf16[64,4096]{1,0:T(8,128)(2,1)} fusion(bf16[1,4096,1024]{2,1,0:T(8,128)(2,1)} %all-gather.5.cloned.1.call-done, bf16[1,4096,1024]{2,1,0:T(8,128)(2,1)} %all-gather.7.cloned.1.call-done, bf16[2,64,4096]{2,1,0:T(8,128)(2,1)S(1)} %copy-done.1, pred[]{:T(512)S(6)} %eq.36, f32[2,64,1024]{2,1,0:T(8,128)} %get-tuple-element.88, s32[]{:T(128)S(6)} %min.22), kind=kOutput, calls=%fused_computation.84 | convolution fusion | flops 1074855936 | bytes 18087940 | tf_op jit(solution)/shard_map/dot_general | solution.py:66
  333.1 73.3 %all-reduce.9.cloned.1.call-done = bf16[64,4096]{1,0:T(8,128)(2,1)} async-done(((bf16[64,4096]{1,0:T(8,128)(2,1)}), bf16[64,4096]{1,0:T(8,128)(2,1)}) %all-reduce.9.cloned.1.call-update) | async-done | bytes 524304 | tf_op jit(solution)/shard_map/psum | solution.py:69
  406.4 1.5 fusion.112
  408.0 1.4 fusion.103
  412.6 9.4 %collective-permute-done.2 = bf16[64,4096]{1,0:T(8,128)(2,1)S(1)} collective-permute-done((bf16[64,4096]{1,0:T(8,128)(2,1)S(1)}, bf16[64,4096]{1,0:T(8,128)(2,1)S(1)}, u32[]{:S(2)}, u32[]{:S(2)}) %collective-permute-start.2) | collective-permute-done | bytes 524320 | tf_op jit(solution)/shard_map/ppermute | solution.py:21
  423.0 11.0 %fusion.69 = bf16[64,4096]{1,0:T(8,128)(2,1)} fusion(bf16[1,4096,1024]{2,1,0:T(8,128)(2,1)} %all-gather.5.cloned.1.call-done, bf16[64,4096]{1,0:T(8,128)(2,1)} %get-tuple-element.69, bf16[1,4096,1024]{2,1,0:T(8,128)(2,1)} %all-gather.7.cloned.1.call-done, f32[2,64,1024]{2,1,0:T(8,128)} %get-tuple-element.88, s32[]{:T(128)S(6)} %min.23), kind=kOutput, calls=%fused_computation.85 | convolution fusion | flops 1074593792 | bytes 18087940 | tf_op jit(solution)/shard_map/dot_general | solution.py:66
  434.4 2.0 gather_fusion
  436.4 3.2 select_bitcast_fusion.1
  439.6 5.7 all-to-all-start
  445.3 59.5 %all-reduce.11.cloned.1.call-done = bf16[64,4096]{1,0:T(8,128)(2,1)} async-done(((bf16[64,4096]{1,0:T(8,128)(2,1)}), bf16[64,4096]{1,0:T(8,128)(2,1)}) %all-reduce.11.cloned.1.call-update) | async-done | bytes 524304 | tf_op jit(solution)/shard_map/psum | solution.py:69
  504.8 1.3 fusion.113
  506.1 2.2 fusion.105
  508.3 1.5 collective-permute-start.3
  509.8 11.3 %collective-permute-done.3 = bf16[64,4096]{1,0:T(8,128)(2,1)S(1)} collective-permute-done((bf16[64,4096]{1,0:T(8,128)(2,1)}, bf16[64,4096]{1,0:T(8,128)(2,1)S(1)}, u32[]{:S(2)}, u32[]{:S(2)}) %collective-permute-start.3) | collective-permute-done | bytes 524320 | tf_op jit(solution)/shard_map/ppermute | solution.py:21
  523.8 1.6 select_bitcast_fusion
  525.4 5.7 all-to-all-start.1
  532.4 27.2 %all-to-all-done.1 = bf16[128,16,512]{2,0,1:T(8,128)(2,1)S(1)} async-done(((bf16[128,16,512]{2,0,1:T(8,128)(2,1)}), bf16[128,16,512]{2,0,1:T(8,128)(2,1)S(1)}, u32[]{:S(2)}, u32[]{:S(2)}) %all-to-all-start.1) | async-done | bytes 2097184 | tf_op jit(solution)/shard_map/all_to_all | solution.py:157
  559.6 4.0 convert_bitcast_fusion
  564.7 2.9 fusion.81
  567.6 2.9 fusion.80
  570.5 35.5 %conditional.1 = (bf16[512,512]{1,0:T(8,128)(2,1)}, bf16[512,512]{1,0:T(8,128)(2,1)}, bf16[1,1,512,512]{3,2,1,0:T(8,128)(2,1)S(1)}, bf16[1,1,512,512]{3,2,1,0:T(8,128)(2,1)S(1)}) conditional(s32[]{:T(128)} %bitcast.42, (bf16[1,1,512,512]{3,2,1,0:T(8,128)(2,1)}, bf16[1,1,512,512]{3,2,1,0:T(8,128)(2,1)}) %tuple.45, (f32[512,512]{1,0:T(8,128)}, ...), branch_computations={%region_13.14_spmd, %region_14.17_spmd} | conditional | flops 16121331712 | bytes 28311688 | solution.py:182
  570.7 2.4 multiply_reduce_fusion
  573.9 3.1 fusion.2
  577.0 3.6 fusion.6
  580.7 1.8 fusion.180
  582.5 3.1 select_subtract_fusion.2
  585.6 2.6 convolution_convert_fusion.1
  589.0 3.1 fusion
  592.1 3.9 fusion.7
  596.0 1.8 fusion.181
  597.9 3.1 select_subtract_fusion
  601.0 2.7 convolution_convert_fusion
  606.1 3.2 fusion.82
  (95 shorter events, 21.3 us)
Async XLA Ops:
  7.2 61.5 %all-gather.5.cloned.1.call-start = ((), (), s32[]{:S(2)}) async-start(), calls=%async_computation.6 | async-start | bytes 8912896 | tf_op jit(solution)/shard_map/all_gather | solution.py:103
  11.0 115.1 %all-gather.7.cloned.1.call-start = ((), (), s32[]{:S(2)}) async-start(), calls=%async_computation.7 | async-start | bytes 8912896 | tf_op jit(solution)/shard_map/all_gather | solution.py:104
  11.7 195.6 %all-reduce.5.cloned.1.call-start = ((), (), s32[]{:S(2)}) async-start(), calls=%async_computation.2 | async-start | bytes 1048576 | tf_op jit(solution)/shard_map/psum | solution.py:58
  73.9 133.5 %copy-start = (bf16[2,64,4096]{2,1,0:T(8,128)(2,1)S(1)}, bf16[2,64,4096]{2,1,0:T(8,128)(2,1)}, u32[]{:S(2)}) copy-start(bf16[2,64,4096]{2,1,0:T(8,128)(2,1)} %param.14) | copy-start | bytes 3145732
  73.9 145.9 %copy-start.7 = (f32[1,4096]{1,0:T(1,128)S(1)}, f32[1,4096]{1,0:T(1,128)}, u32[]{:S(2)}) copy-start(f32[1,4096]{1,0:T(1,128)} %param.16) | copy-start | bytes 49156
  132.9 170.3 %all-reduce.7.cloned.1.call-start = ((), (), s32[]{:S(2)}) async-start(), calls=%async_computation.3 | async-start | bytes 1048576 | tf_op jit(solution)/shard_map/psum | solution.py:58
  208.6 10.7 %collective-permute-start = (bf16[64,4096]{1,0:T(8,128)(2,1)S(1)}, bf16[64,4096]{1,0:T(8,128)(2,1)S(1)}, u32[]{:S(2)}, u32[]{:S(2)}) collective-permute-start(bf16[64,4096]{1,0:T(8,128)(2,1)S(1)} %fusion.109), channel_id=1, source_target_pairs={{0,128},{1,129},{2,130},{3,131},{4,132},{5,133},{6,134},{7,135},{8... | collective-permute-start | bytes 1572872 | tf_op jit(solution)/shard_map/ppermute | solution.py:21
  219.5 6.1 slice-start
  219.8 5.9 slice-start.1
  225.0 0.7 copy-start.4
  225.0 79.5 %copy-start.2 = (f32[2,64,1024]{2,1,0:T(8,128)}, f32[2,64,1024]{2,1,0:T(8,128)S(1)}, u32[]{:S(2)}) copy-start(f32[2,64,1024]{2,1,0:T(8,128)S(1)} %get-tuple-element.86) | copy-start | bytes 1572868
  225.0 4.9 copy-start.13
  225.0 4.9 copy-start.14
  229.2 177.3 %all-reduce.9.cloned.1.call-start = ((), (), s32[]{:S(2)}) async-start(), calls=%async_computation.4 | async-start | bytes 1048576 | tf_op jit(solution)/shard_map/psum | solution.py:69
  304.4 10.7 %collective-permute-start.1 = (bf16[64,4096]{1,0:T(8,128)(2,1)S(1)}, bf16[64,4096]{1,0:T(8,128)(2,1)S(1)}, u32[]{:S(2)}, u32[]{:S(2)}) collective-permute-start(bf16[64,4096]{1,0:T(8,128)(2,1)S(1)} %fusion.101), channel_id=1, source_target_pairs={{0,128},{1,129},{2,130},{3,131},{4,132},{5,133},{6,134},{7,135},{8... | collective-permute-start | bytes 1572872 | tf_op jit(solution)/shard_map/ppermute | solution.py:21
  315.6 5.9 copy-start.1
  332.4 172.4 %all-reduce.11.cloned.1.call-start = ((), (), s32[]{:S(2)}) async-start(), calls=%async_computation.5 | async-start | bytes 1048576 | tf_op jit(solution)/shard_map/psum | solution.py:69
  409.4 12.6 %collective-permute-start.2 = (bf16[64,4096]{1,0:T(8,128)(2,1)S(1)}, bf16[64,4096]{1,0:T(8,128)(2,1)S(1)}, u32[]{:S(2)}, u32[]{:S(2)}) collective-permute-start(bf16[64,4096]{1,0:T(8,128)(2,1)S(1)} %fusion.103), channel_id=1, source_target_pairs={{128,0},{129,1},{130,2},{131,3},{132,4},{133,5},{134,6},{135,7},{1... | collective-permute-start | bytes 1572872 | tf_op jit(solution)/shard_map/ppermute | solution.py:21
  411.9 0.7 copy-start.5
  423.0 11.0 %copy-start.6 = (bf16[2,64,1024]{2,1,0:T(8,128)(2,1)S(1)}, bf16[2,64,1024]{2,1,0:T(8,128)(2,1)}, u32[]{:S(2)}) copy-start(bf16[2,64,1024]{2,1,0:T(8,128)(2,1)} %copy-done.5) | copy-start | bytes 786436
  423.0 11.0 %copy-start.8 = (f32[64,1024]{1,0:T(8,128)S(1)}, f32[64,1024]{1,0:T(8,128)}, u32[]{:S(2)}) copy-start(f32[64,1024]{1,0:T(8,128)} %get-tuple-element.89) | copy-start | bytes 786436
  434.0 72.1 %copy-start.3 = (bf16[64,4096]{1,0:T(8,128)(2,1)S(1)}, bf16[64,4096]{1,0:T(8,128)(2,1)}, u32[]{:S(2)}) copy-start(bf16[64,4096]{1,0:T(8,128)(2,1)} %get-tuple-element.69) | copy-start | bytes 1572868
  439.6 85.8 %all-to-all-start = ((bf16[128,16,512]{2,0,1:T(8,128)(2,1)}), bf16[128,16,512]{2,0,1:T(8,128)(2,1)}, u32[]{:S(2)}, u32[]{:S(2)}) async-start(bf16[128,16,512]{2,0,1:T(8,128)(2,1)} %select_bitcast_fusion.1), calls=%async_computation | async-start | bytes 4194304 | tf_op jit(solution)/shard_map/all_to_all | solution.py:156
  508.3 12.8 %collective-permute-start.3 = (bf16[64,4096]{1,0:T(8,128)(2,1)}, bf16[64,4096]{1,0:T(8,128)(2,1)S(1)}, u32[]{:S(2)}, u32[]{:S(2)}) collective-permute-start(bf16[64,4096]{1,0:T(8,128)(2,1)} %fusion.105), channel_id=1, source_target_pairs={{128,0},{129,1},{130,2},{131,3},{132,4},{133,5},{134,6},{135,7},{1... | collective-permute-start | bytes 1572872 | tf_op jit(solution)/shard_map/ppermute | solution.py:21
  525.4 34.1 %all-to-all-start.1 = ((bf16[128,16,512]{2,0,1:T(8,128)(2,1)}), bf16[128,16,512]{2,0,1:T(8,128)(2,1)S(1)}, u32[]{:S(2)}, u32[]{:S(2)}) async-start(bf16[128,16,512]{2,0,1:T(8,128)(2,1)} %select_bitcast_fusion), calls=%async_computation.1 | async-start | bytes 4194304 | tf_op jit(solution)/shard_map/all_to_all | solution.py:157
  532.4 32.4 %copy-start.9 = (f32[1,1,512,512]{3,2,1,0:T(8,128)S(1)}, f32[1,1,512,512]{3,2,1,0:T(8,128)}, u32[]{:S(2)}) copy-start(f32[1,1,512,512]{3,2,1,0:T(8,128)} %param.19) | copy-start | bytes 3145732
  563.5 4.1 copy-start.10
  606.0 3.2 copy-start.11
  606.0 3.2 copy-start.12
Sparse Core Ops, SparseCore 0:
  11.1 57.4 all-gather.4
  70.5 55.5 all-gather.6
  133.0 74.2 all-reduce.4
  229.3 73.9 all-reduce.6
  332.5 73.8 all-reduce.8
  434.2 70.5 all-reduce.10
where the time goes:
time: 624 us; the launch traced here: 617 us
  waiting for transfers between devices  446 us (71%)
  matrix products  90.3 us (14%)
  other arithmetic  25.6 us (4%)
  starting transfers between devices  23.1 us (4%)
  between operations  16.4 us (3%)
  local copies, waits for them, and re-layouts  12.8 us (2%)
    psum x2, waiting for transfers between devices, forward_layer(): lax.psum(partial_value.astype(jnp.bfloat16), 'mp').astype(jnp.float32)  146 us
    psum x2, waiting for transfers between devices, backward_layer(): lax.psum(partial_value.astype(jnp.bfloat16), 'mp').astype(jnp.float32)  133 us
    all_gather x1, waiting for transfers between devices, on_device(): lax.all_gather(w_up[0], 'dp', axis=0, tiled=True)  55.5 us
    all_gather x1, waiting for transfers between devices, on_device(): lax.all_gather(w_down[0], 'dp', axis=0, tiled=True)  52.1 us
    ppermute x4, waiting for transfers between devices, passed_along(): return lax.ppermute(block, axis, route)  31.9 us
    all_to_all x1, waiting for transfers between devices, on_device(): lax.all_to_all(grad_slots, 'dp', split_axis=1, concat_axis=0, tiled=True)  27.2 us
    dot_general x2, matrix products, backward_layer(): lax.dot_general(grad_pre, up_rows, (((1,), (1,)), ((), ())), preferred_el...  21.8 us
    dot_general x3, matrix products, forward_layer(): pre_act = jnp.dot(normed, up_rows, preferred_element_type=jnp.float32)  16.3 us
  transfers between devices with their start and end apart: 12, of which 11 were waited for; matrix products, arithmetic and copies ran while one was open for 4% of the time, Pallas kernels for 0%

commit v1 on v0

v1 whole, which is shorter than its diff:
```python
import functools
import math

import jax
import jax.numpy as jnp
from jax import lax
from jax.experimental import pallas as pl
from jax.experimental.pallas import tpu as pltpu
from jax.sharding import PartitionSpec as P

BLK = 512
ITERS = 2

norm_epsilon = 1e-05
decay_rate = 0.9
ridge_shift = 0.001
f32 = jnp.float32
bf16 = jnp.bfloat16


def normalize_values(values, gain_row):
    inverse_rms = lax.rsqrt(jnp.mean(values * values, axis=-1, keepdims=True) + norm_epsilon)
    return values * inverse_rms * gain_row


def silu_slope(pre_act):
    sigmoid_values = jax.nn.sigmoid(pre_act)
    return sigmoid_values * (1.0 + pre_act * (1.0 - sigmoid_values))


def dot(a, b, dims=((1,), (0,))):
    return lax.dot_general(a, b, (dims, ((), ())), preferred_element_type=f32)


def early_kernel(block_cols, info_ref, hidden_ref, cot_ref, o_ref):
    slots = o_ref.shape[0]

    @pl.when(info_ref[0] == 0)
    def _():
        for t in range(slots):
            at = pl.multiple_of((info_ref[2 + t] // block_cols) * BLK, BLK)
            o_ref[t] = hidden_ref[:, pl.ds(at, BLK)]

    @pl.when(info_ref[0] != 0)
    def _():
        for t in range(slots):
            at = pl.multiple_of((info_ref[2 + t] % block_cols) * BLK, BLK)
            o_ref[t] = cot_ref[:, pl.ds(at, BLK)]


def late_kernel(block_cols, info_ref, hidden_ref, *refs):
    chunks, o_ref = refs[:-1], refs[-1]
    slots = o_ref.shape[0]
    count, share = len(chunks), chunks[0].shape[0]

    @pl.when(info_ref[0] == 0)
    def _():
        for k in range(count):
            place = pl.multiple_of(((info_ref[1] + count - k) % count) * share, share)
            for t in range(slots):
                at = pl.multiple_of((info_ref[2 + t] % block_cols) * BLK, BLK)
                o_ref[t, pl.ds(place, share), :] = chunks[k][:, pl.ds(at, BLK)]

    @pl.when(info_ref[0] != 0)
    def _():
        for t in range(slots):
            at = pl.multiple_of((info_ref[2 + t] // block_cols) * BLK, BLK)
            o_ref[t] = hidden_ref[:, pl.ds(at, BLK)]


def place_kernel(info_ref, *refs):
    chunks, o_ref = refs[:-1], refs[-1]
    count, share = len(chunks), chunks[0].shape[0]
    for k in range(count):
        place = pl.multiple_of(((info_ref[1] + count - k) % count) * share, share)
        o_ref[pl.ds(place, share), :] = chunks[k][...]


def whole(kernel, name, shape, info, *arrays):
    vmem = pl.BlockSpec(memory_space=pltpu.VMEM)
    return pl.pallas_call(
        kernel,
        in_specs=[pl.BlockSpec(memory_space=pltpu.SMEM)] + [vmem] * len(arrays),
        out_specs=vmem,
        out_shape=jax.ShapeDtypeStruct(shape, bf16),
        compiler_params=pltpu.CompilerParams(vmem_limit_bytes=40 * 1024 * 1024),
        name=name,
    )(info, *arrays)


def inverse_root(matrix):
    order = matrix.shape[-1]
    row = lax.broadcasted_iota(jnp.int32, (order, order), 0)
    col = lax.broadcasted_iota(jnp.int32, (order, order), 1)
    diag = row == col
    shifted = matrix + jnp.where(diag, ridge_shift, 0.0)
    factor = 2.5 / jnp.sqrt(jnp.sum(shifted * shifted))
    moment = factor * shifted
    step = jnp.where(diag, 1.25, 0.0) - 0.25 * moment
    low = step.astype(bf16)
    square = dot(low, low).astype(bf16)
    fourth = dot(square, square).astype(bf16)
    moment = dot(fourth, moment.astype(bf16))
    last = jnp.where(diag, 1.25, 0.0) - 0.25 * moment
    root = jnp.sqrt(jnp.sqrt(factor))
    return root * dot(low, last.astype(bf16))


def owner_kernel(scale, info_ref, early_ref, late_ref, gl_ref, gr_ref, rl_ref, rr_ref,
                 ngl_ref, ngr_ref, nrl_ref, nrr_ref, up_ref, grad_ref):
    @pl.when(info_ref[0] == 0)
    def _():
        grad_ref[...] = dot(early_ref[...], late_ref[...], ((0,), (0,))) * scale

    @pl.when(info_ref[0] != 0)
    def _():
        grad_ref[...] = dot(late_ref[...], early_ref[...], ((0,), (0,))) * scale

    grad = grad_ref[...]
    low = grad.astype(bf16)
    ngl_ref[...] = decay_rate * gl_ref[...] + dot(low, low, ((1,), (1,))) * (1.0 / BLK)
    ngr_ref[...] = decay_rate * gr_ref[...] + dot(low, low, ((0,), (0,))) * (1.0 / BLK)
    nrl_ref[...] = rl_ref[...]
    nrr_ref[...] = rr_ref[...]

    @pl.when(info_ref[1] == 1)
    def _():
        nrl_ref[...] = inverse_root(ngl_ref[...]).astype(bf16)
        nrr_ref[...] = inverse_root(ngr_ref[...]).astype(bf16)

    right = dot(low, nrr_ref[...]).astype(bf16)
    up_ref[...] = dot(nrl_ref[...], right).astype(bf16)


def owner_step(scale, info, early, late, gram_l, gram_r, root_l, root_r):
    vmem = pl.BlockSpec(memory_space=pltpu.VMEM)
    big = jax.ShapeDtypeStruct((BLK, BLK), f32)
    small = jax.ShapeDtypeStruct((BLK, BLK), bf16)
    return pl.pallas_call(
        functools.partial(owner_kernel, scale),
        in_specs=[pl.BlockSpec(memory_space=pltpu.SMEM)] + [vmem] * 6,
        out_specs=[vmem] * 5,
        out_shape=[big, big, small, small, small],
        scratch_shapes=[pltpu.VMEM((BLK, BLK), f32)],
        compiler_params=pltpu.CompilerParams(vmem_limit_bytes=40 * 1024 * 1024),
        name="owner_step",
    )(info, early, late, gram_l, gram_r, root_l, root_r)


def on_device(
    activations,
    cotangent,
    norm_gain,
    w_up,
    w_down,
    gram_left,
    gram_right,
    root_left,
    root_right,
    owner_slot,
    eighth,
    refresh_phase,
):
    section_no = lax.axis_index("section")
    dp_no = lax.axis_index("dp")
    mp_no = lax.axis_index("mp")
    core = dp_no % 2
    dp_count = lax.axis_size("dp")
    mp_count = lax.axis_size("mp")
    micro_count, row_count, width = activations.shape
    tokens = micro_count * row_count
    share = tokens // mp_count
    chips = dp_count // 2
    depth, shard_ff = w_up.shape[1:]
    half = shard_ff // 2
    gain_row = norm_gain[0]
    is_first = section_no == 0
    on_low_core = core == 0
    same_core = [[2 * q + c for q in range(chips)] for c in range(2)]
    swap_cores = [(i, i ^ 1) for i in range(dp_count)]

    first = jnp.where(is_first, w_up[0], w_down[0])
    second = jnp.where(is_first, w_down[0], w_up[0])
    second_full = lax.all_gather(second, "dp", axis=0, tiled=True)

    act = activations.reshape(tokens, width)
    cot = cotangent.reshape(tokens, width)
    normed = normalize_values(act.astype(f32), gain_row).astype(bf16)
    operand = jnp.where(is_first, normed, cot)

    kept = jnp.where(on_low_core, first[:, :half], first[:, half:])
    given = jnp.where(on_low_core, first[:, half:], first[:, :half])
    taken = lax.ppermute(given, "dp", swap_cores)
    chip_rows = jnp.concatenate(
        [jnp.where(on_low_core, kept, taken), jnp.where(on_low_core, taken, kept)], axis=0
    )

    cut = operand.reshape(tokens, chips, 2 * depth).transpose(1, 0, 2)
    own = lax.all_to_all(
        cut, "dp", split_axis=0, concat_axis=0, axis_index_groups=same_core, tiled=True
    )
    other = lax.ppermute(own, "dp", swap_cores)
    own_product = dot(own.reshape(chips * tokens, 2 * depth), chip_rows).astype(bf16)
    other_product = dot(other.reshape(chips * tokens, 2 * depth), chip_rows).astype(bf16)
    own_product = own_product.reshape(chips, 1, tokens, half)
    other_product = other_product.reshape(chips, 1, tokens, half)
    to_replicas = jnp.concatenate(
        [
            jnp.where(on_low_core, own_product, other_product),
            jnp.where(on_low_core, other_product, own_product),
        ],
        axis=1,
    ).reshape(dp_count, tokens, half)
    parts = lax.all_to_all(to_replicas, "dp", split_axis=0, concat_axis=0, tiled=True)
    halves = jnp.sum(parts.reshape(chips, 2, tokens, half).astype(f32), axis=0)
    product = jnp.concatenate([halves[0], halves[1]], axis=1)
    hidden_first = jax.nn.silu(product).astype(bf16)

    def sum_over_mp(partial_value):
        pieces = lax.all_to_all(
            partial_value.reshape(mp_count, share, width), "mp",
            split_axis=0, concat_axis=0, tiled=True,
        )
        return jnp.sum(pieces.astype(f32), axis=0)

    def ring_over_mp(rows):
        right = [(i, (i + 1) % mp_count) for i in range(mp_count)]
        left = [((i + 1) % mp_count, i) for i in range(mp_count)]
        behind, ahead = [rows], []
        for step in range(mp_count // 2):
            behind.append(lax.ppermute(behind[-1], "mp", right))
            if step < mp_count // 2 - 1:
                ahead.append(lax.ppermute(ahead[-1] if ahead else rows, "mp", left))
        return behind + ahead[::-1]

    block_rows = shard_ff // BLK
    block_cols = width // BLK
    group_size = block_rows * block_cols
    section_owner = lax.dynamic_index_in_dim(owner_slot, section_no, 0, keepdims=False)
    local_owner = lax.dynamic_slice_in_dim(
        section_owner, mp_no * block_rows, block_rows, 0
    ).reshape(-1)
    local_slot = local_owner // mp_count
    slots = jnp.arange(group_size, dtype=jnp.int32)
    block_of_slot = jnp.sum(
        jnp.where(local_slot[None, :] == slots[:, None], slots[None, :], 0), axis=1
    )
    info = jnp.concatenate([jnp.stack([section_no, mp_no]).astype(jnp.int32), block_of_slot])

    def to_owners(blocks):
        return lax.all_to_all(blocks, "dp", split_axis=0, concat_axis=0, tiled=True)

    slot_shape = (group_size, tokens, BLK)
    early_blocks = whole(
        functools.partial(early_kernel, block_cols), "early_blocks", slot_shape, info, hidden_first, cot
    )

    partial_out = dot(hidden_first, second_full, ((1,), (1,))).astype(bf16)
    my_rows = functools.partial(
        lax.dynamic_slice_in_dim, start_index=mp_no * share, slice_size=share, axis=0
    )
    output = (my_rows(act).astype(f32) + sum_over_mp(partial_out)).astype(bf16)
    layer_in = lax.ppermute(output, "section", [(0, 1)])
    early_blocks, layer_in = lax.optimization_barrier((early_blocks, layer_in))
    early = to_owners(early_blocks)
    values = layer_in.astype(f32)
    normed_rows, pullback = jax.vjp(lambda v: normalize_values(v, gain_row), values)
    chunks = ring_over_mp(normed_rows.astype(bf16))
    normed_second = whole(place_kernel, "place", (tokens, width), info, *chunks)
    normed_second, early = lax.optimization_barrier((normed_second, early))
    pre_act = dot(normed_second, second_full)
    hidden_second = jax.nn.silu(pre_act).astype(bf16)

    grad_pre = (product * silu_slope(pre_act)).astype(bf16)
    partial_grad = dot(grad_pre, second_full, ((1,), (1,))).astype(bf16)
    grad_normed = sum_over_mp(partial_grad)
    grad_in = (my_rows(cot).astype(f32) + pullback(grad_normed)[0]).astype(bf16)
    grad_out = lax.ppermute(grad_in, "section", [(1, 0)])
    chunks = ring_over_mp(grad_out)
    late_blocks = whole(
        functools.partial(late_kernel, block_cols), "late_blocks", slot_shape, info,
        hidden_second, *chunks,
    )
    late = to_owners(late_blocks)

    section_eighth = lax.dynamic_index_in_dim(eighth, section_no, 0, keepdims=False)
    local_eighth = lax.dynamic_slice_in_dim(
        section_eighth, mp_no * block_rows, block_rows, 0
    ).reshape(-1)
    my_eighth = jnp.sum(jnp.where(local_slot == dp_no, local_eighth, 0))
    due = (my_eighth == refresh_phase[0] % 8).astype(jnp.int32)
    outs = owner_step(
        1.0 / math.sqrt(tokens * dp_count), jnp.stack([section_no.astype(jnp.int32), due]),
        early.reshape(dp_count * tokens, BLK), late.reshape(dp_count * tokens, BLK),
        gram_left[0, 0], gram_right[0, 0], root_left[0, 0], root_right[0, 0],
    )
    return tuple(o[None, None] for o in outs)


def solution(mesh):
    spread = P("section", ("dp", "mp"), None, None)
    return jax.shard_map(
        on_device,
        mesh=mesh,
        in_specs=(
            P(None, "dp", None),
            P(None, "dp", None),
            P("section", None),
            P("section", "dp", "mp"),
            P("section", "dp", "mp"),
            spread,
            spread,
            spread,
            spread,
            P(),
            P(),
            P(),
        ),
        out_specs=(spread,) * 5,
        check_vma=False,
    )
```

time: 624 us -> 314 us (0.50)
  waiting for transfers between devices: 446 us -> 99.9 us
  blocking collectives: 0 us -> 104 us
  matrix products: 90.3 us -> 22.4 us
  starting transfers between devices: 23.1 us -> 44.2 us
  other arithmetic: 25.6 us -> 6.27 us
  Pallas kernels: 0 us -> 10.6 us
    psum x4 -> x0, waiting for transfers between devices: 279 us -> none  [the longest x2 146 us: forward_layer(): lax.psum(partial_value.astype(jnp.bfloat16), 'mp').astype(jnp.float32)]
    all_gather x2 -> x1, waiting for transfers between devices: 108 us -> 0.58 us  [on_device(): second_full = lax.all_gather(second, 'dp', axis=0, tiled=True)]
    all_to_all x0 -> x3, blocking collectives: none -> 104 us  [the longest x1 47.6 us: on_device(): lax.all_to_all(to_replicas, 'dp', split_axis=0, concat_axis=0, tiled=True)]
    dot_general x21 -> x5, matrix products: 90.3 us -> 22.4 us  [dot(): return lax.dot_general(a, b, (dims, ((), ())), preferred_element_type=f32)]
    all_to_all x2 -> x3, waiting for transfers between devices: 27.2 us -> 56.6 us  [the longest x2 28.4 us: to_owners(): return lax.all_to_all(blocks, 'dp', split_axis=0, concat_axis=0, tiled=True)]
    ppermute x4 -> x18, starting transfers between devices: 11.4 us -> 25.9 us  [the longest x6 19 us: ring_over_mp(): ahead.append(lax.ppermute(ahead[-1] if ahead else rows, 'mp', left))]
    ppermute x4 -> x18, waiting for transfers between devices: 31.9 us -> 42.7 us  [the longest x8 32.5 us: ring_over_mp(): behind.append(lax.ppermute(behind[-1], 'mp', right))]
    pallas_call x0 -> x4, Pallas kernels: none -> 10.6 us  [the longest x1 5.73 us: owner_step(): pl.pallas_call(functools.partial(owner_kernel, scale), in_specs=[pl.Block...]
  transfers between devices with their start and end apart: 12 -> 22, of which waited for: 11 -> 15; matrix products, arithmetic and copies ran while one was open for 4% -> 3% of each run, Pallas kernels for 0% -> 1%
where the time goes in v1:
time: 314 us; the launch traced here: 310 us
  blocking collectives  104 us (33%)
  waiting for transfers between devices  99.9 us (32%)
  starting transfers between devices  44.2 us (14%)
  matrix products  22.4 us (7%)
  between operations  15.6 us (5%)
  Pallas kernels  10.6 us (3%)
  local copies, waits for them, and re-layouts  7.02 us (2%)
  other arithmetic  6.27 us (2%)
    all_to_all x1, blocking collectives, on_device(): lax.all_to_all(to_replicas, 'dp', split_axis=0, concat_axis=0, tiled=True)  47.6 us
    ppermute x8, waiting for transfers between devices, ring_over_mp(): behind.append(lax.ppermute(behind[-1], 'mp', right))  32.5 us
    all_to_all x1, blocking collectives, sum_over_mp(): lax.all_to_all(partial_value.reshape(mp_count, share, width), 'mp', split...  31.2 us
    all_to_all x2, waiting for transfers between devices, to_owners(): return lax.all_to_all(blocks, 'dp', split_axis=0, concat_axis=0, tiled=True)  28.4 us
    all_to_all x1, waiting for transfers between devices, sum_over_mp(): lax.all_to_all(partial_value.reshape(mp_count, share, width), 'mp', split...  28.2 us
    all_to_all x1, blocking collectives, on_device(): lax.all_to_all(cut, 'dp', split_axis=0, concat_axis=0, axis_index_groups=...  25.1 us
    dot_general x5, matrix products, dot(): return lax.dot_general(a, b, (dims, ((), ())), preferred_element_type=f32)  22.4 us
    ppermute x6, starting transfers between devices, ring_over_mp(): ahead.append(lax.ppermute(ahead[-1] if ahead else rows, 'mp', left))  19 us
  transfers between devices with their start and end apart: 22, of which 15 were waited for; matrix products, arithmetic and copies ran while one was open for 3% of the time, Pallas kernels for 1%

profile of v1, /device:TPU:10, one launch (start us, length us, event | category | flops | bytes accessed | tf_op | source)
XLA Modules:
  0.0 310.0 jit_solution(6385214921514408827)
XLA Ops:
  7.3 2.2 broadcast_select_fusion.2
  10.4 0.7 reduce.5
  12.7 25.1 %all_to_all.30 = bf16[8,128,512]{2,1,0:T(8,128)(2,1)} all-to-all(bf16[8,128,512]{2,1,0:T(8,128)(2,1)S(1)} %copy.31), channel_id=1, replica_groups={{0,16,32,48,64,80,96,112},{8,24,40,56,72,88,104,120},{1,17,33,49,65,81,..., dimensions={0} | all-to-all | bytes 2097152 | tf_op jit(solution)/shard_map/all_to_all | solution.py:199
  37.8 0.6 collective-permute-start
  38.4 2.5 collective-permute-done
  41.0 1.9 convolution_convert_fusion
  43.0 2.0 broadcast_select_fusion.1
  45.2 47.6 %all_to_all.31 = bf16[16,128,512]{2,1,0:T(8,128)(2,1)S(1)} all-to-all(bf16[16,128,512]{2,1,0:T(8,128)(2,1)S(1)} %bitcast.82), channel_id=1, replica_groups=mesh['section'=2,'dp'=16,'mp'=8] {'dp'}, dimensions={0} | all-to-all | bytes 4194304 | tf_op jit(solution)/shard_map/all_to_all | solution.py:214
  93.1 0.7 copy-done.7
  94.0 0.6 all-gather.3.cloned.1.call-done
  94.6 7.2 %fusion.6 = bf16[128,4096]{1,0:T(8,128)(2,1)} fusion(bf16[128,1024]{1,0:T(8,128)(2,1)S(1)} %multiply_convert_fusion.2.hidden_ref, bf16[1,4096,1024]{2,1,0:T(8,128)(2,1)} %all-gather.3.cloned.1.call-done), kind=kOutput, calls=%fused_computation.6 | convolution fusion | flops 1074266112 | bytes 9699328 | tf_op jit(solution)/shard_map/dot_general | solution.py:32
  101.9 8.6 %all-to-all-start.2 = ((bf16[8,16,4096]{2,1,0:T(8,128)(2,1)}), bf16[8,16,4096]{2,1,0:T(8,128)(2,1)S(1)}, u32[]{:S(2)}, u32[]{:S(2)}) async-start(bf16[8,16,4096]{2,1,0:T(8,128)(2,1)} %bitcast.19), calls=%async_computation.2 | async-start | bytes 2097152 | tf_op jit(solution)/shard_map/all_to_all | solution.py:220
  110.5 0.8 constant_dynamic-slice_fusion
  111.4 28.2 %all-to-all-done.2 = bf16[8,16,4096]{2,1,0:T(8,128)(2,1)S(1)} async-done(((bf16[8,16,4096]{2,1,0:T(8,128)(2,1)}), bf16[8,16,4096]{2,1,0:T(8,128)(2,1)S(1)}, u32[]{:S(2)}, u32[]{:S(2)}) %all-to-all-start.2) | async-done | bytes 1048608 | tf_op jit(solution)/shard_map/all_to_all | solution.py:220
  139.8 4.2 %collective-permute-start.2 = (bf16[16,4096]{1,0:T(8,128)(2,1)S(1)}, bf16[16,4096]{1,0:T(8,128)(2,1)S(1)}, u32[]{:S(2)}, u32[]{:S(2)}) collective-permute-start(bf16[16,4096]{1,0:T(8,128)(2,1)S(1)} %add_convert_fusion), channel_id=1, source_target_pairs={{0,128},{1,129},{2,130},{3,131},{4,132},{5,133},{6,134},{7,135},{8... | collective-permute-start | bytes 393224 | tf_op jit(solution)/shard_map/ppermute | solution.py:263
  144.2 2.1 early_blocks.1
  146.3 0.6 collective-permute-done.2
  147.0 5.1 %all-to-all-start.3 = ((bf16[16,128,512]{2,1,0:T(8,128)(2,1)}), bf16[16,128,512]{2,1,0:T(8,128)(2,1)S(1)}, u32[]{:S(2)}, u32[]{:S(2)}) async-start(bf16[16,128,512]{2,1,0:T(8,128)(2,1)} %early_blocks.1), calls=%async_computation.3 | async-start | bytes 4194304 | tf_op jit(solution)/shard_map/all_to_all | solution.py:251
  152.5 3.1 %collective-permute-start.7 = (bf16[16,4096]{1,0:T(8,128)(2,1)S(1)}, bf16[16,4096]{1,0:T(8,128)(2,1)S(1)}, u32[]{:S(2)}, u32[]{:S(2)}) collective-permute-start(bf16[16,4096]{1,0:T(8,128)(2,1)S(1)} %fusion.19.refs_0_), channel_id=1, source_target_pairs={{1,0},{2,1},{3,2},{4,3},{5,4},{6,5},{7,6},{0,7},{9,8},{10,9},{11,1... | collective-permute-start | bytes 393224 | tf_op jit(solution)/shard_map/ppermute | solution.py:233
  155.6 3.5 %collective-permute-done.3.refs_1_ = bf16[16,4096]{1,0:T(8,128)(2,1)S(1)} collective-permute-done((bf16[16,4096]{1,0:T(8,128)(2,1)S(1)}, bf16[16,4096]{1,0:T(8,128)(2,1)S(1)}, u32[]{:S(2)}, u32[]{:S(2)}) %collective-permute-start.3) | collective-permute-done | bytes 131104 | tf_op jit(solution)/shard_map/ppermute | solution.py:231
  159.1 3.2 %collective-permute-start.8 = (bf16[16,4096]{1,0:T(8,128)(2,1)S(1)}, bf16[16,4096]{1,0:T(8,128)(2,1)S(1)}, u32[]{:S(2)}, u32[]{:S(2)}) collective-permute-start(bf16[16,4096]{1,0:T(8,128)(2,1)S(1)} %collective-permute-done.7.refs_7_), channel_id=1, source_target_pairs={{1,0},{2,1},{3,2},{4,3},{5,4},{6,5},{7,6},{0,7},{9,8},{10,9},{11,1... | collective-permute-start | bytes 393224 | tf_op jit(solution)/shard_map/ppermute | solution.py:233
  162.4 2.9 collective-permute-done.4.refs_2_
  165.3 3.2 %collective-permute-start.9 = (bf16[16,4096]{1,0:T(8,128)(2,1)S(1)}, bf16[16,4096]{1,0:T(8,128)(2,1)S(1)}, u32[]{:S(2)}, u32[]{:S(2)}) collective-permute-start(bf16[16,4096]{1,0:T(8,128)(2,1)S(1)} %collective-permute-done.8.refs_6_), channel_id=1, source_target_pairs={{1,0},{2,1},{3,2},{4,3},{5,4},{6,5},{7,6},{0,7},{9,8},{10,9},{11,1... | collective-permute-start | bytes 393224 | tf_op jit(solution)/shard_map/ppermute | solution.py:233
  168.5 2.9 collective-permute-done.5.refs_3_
  171.5 6.2 %collective-permute-done.6.refs_4_ = bf16[16,4096]{1,0:T(8,128)(2,1)S(1)} collective-permute-done((bf16[16,4096]{1,0:T(8,128)(2,1)S(1)}, bf16[16,4096]{1,0:T(8,128)(2,1)S(1)}, u32[]{:S(2)}, u32[]{:S(2)}) %collective-permute-start.6) | collective-permute-done | bytes 131104 | tf_op jit(solution)/shard_map/ppermute | solution.py:231
  177.7 0.6 place.1
  178.3 1.0 copy-done.1
  179.3 1.2 all-to-all-done.3
  180.5 5.1 %multiply_convert_fusion.1 = (bf16[128,1024]{1,0:T(8,128)(2,1)S(1)}, f32[128,1024]{1,0:T(8,128)S(1)}) fusion(bf16[128,4096]{1,0:T(8,128)(2,1)} %copy-done.1, bf16[1,4096,1024]{2,1,0:T(8,128)(2,1)} %all-gather.3.cloned.1.call-done), kind=kOutput, calls=%fused_computation.24 | convolution fusion | flops 1074397184 | bytes 10223616 | tf_op jit(solution)/shard_map/dot_general | solution.py:32
  185.6 6.2 %fusion.9 = bf16[128,4096]{1,0:T(8,128)(2,1)S(1)} fusion(bf16[1,4096,1024]{2,1,0:T(8,128)(2,1)} %all-gather.3.cloned.1.call-done, f32[128,1024]{1,0:T(8,128)S(1)} %get-tuple-element.34, f32[128,512]{1,0:T(8,128)S(1)} %copy-done.10, f32[128,512]{1,0:T(8,128)S(1)} %copy-done.8), kind=kOutput, calls=%fused_computation.7 | convolution fusion | flops 1075576832 | bytes 10485760 | tf_op jit(solution)/shard_map/dot_general | solution.py:32
  191.8 31.2 %all_to_all.32 = bf16[8,16,4096]{2,1,0:T(8,128)(2,1)S(1)} all-to-all(bf16[8,16,4096]{2,1,0:T(8,128)(2,1)S(1)} %bitcast.86), channel_id=1, replica_groups=mesh['section'=2,'dp'=16,'mp'=8] {'mp'}, dimensions={0} | all-to-all | bytes 2097152 | tf_op jit(solution)/shard_map/all_to_all | solution.py:220
  223.5 1.3 collective-permute-start.10
  224.8 7.1 %collective-permute-done.10.refs_0_ = bf16[16,4096]{1,0:T(8,128)(2,1)S(1)} collective-permute-done((bf16[16,4096]{1,0:T(8,128)(2,1)S(1)}, bf16[16,4096]{1,0:T(8,128)(2,1)S(1)}, u32[]{:S(2)}, u32[]{:S(2)}) %collective-permute-start.10) | collective-permute-done | bytes 131104 | tf_op jit(solution)/shard_map/ppermute | solution.py:278
  231.9 0.6 collective-permute-start.11
  232.4 2.7 collective-permute-start.15
  235.1 3.2 %collective-permute-done.11.refs_1_ = bf16[16,4096]{1,0:T(8,128)(2,1)S(1)} collective-permute-done((bf16[16,4096]{1,0:T(8,128)(2,1)S(1)}, bf16[16,4096]{1,0:T(8,128)(2,1)S(1)}, u32[]{:S(2)}, u32[]{:S(2)}) %collective-permute-start.11) | collective-permute-done | bytes 131104 | tf_op jit(solution)/shard_map/ppermute | solution.py:231
  238.3 3.5 %collective-permute-start.16 = (bf16[16,4096]{1,0:T(8,128)(2,1)S(1)}, bf16[16,4096]{1,0:T(8,128)(2,1)S(1)}, u32[]{:S(2)}, u32[]{:S(2)}) collective-permute-start(bf16[16,4096]{1,0:T(8,128)(2,1)S(1)} %collective-permute-done.15.refs_7_), channel_id=1, source_target_pairs={{1,0},{2,1},{3,2},{4,3},{5,4},{6,5},{7,6},{0,7},{9,8},{10,9},{11,1... | collective-permute-start | bytes 393224 | tf_op jit(solution)/shard_map/ppermute | solution.py:233
  241.9 4.0 %collective-permute-done.12.refs_2_ = bf16[16,4096]{1,0:T(8,128)(2,1)S(1)} collective-permute-done((bf16[16,4096]{1,0:T(8,128)(2,1)S(1)}, bf16[16,4096]{1,0:T(8,128)(2,1)S(1)}, u32[]{:S(2)}, u32[]{:S(2)}) %collective-permute-start.12) | collective-permute-done | bytes 131104 | tf_op jit(solution)/shard_map/ppermute | solution.py:231
  245.9 3.2 %collective-permute-start.17 = (bf16[16,4096]{1,0:T(8,128)(2,1)S(1)}, bf16[16,4096]{1,0:T(8,128)(2,1)S(1)}, u32[]{:S(2)}, u32[]{:S(2)}) collective-permute-start(bf16[16,4096]{1,0:T(8,128)(2,1)S(1)} %collective-permute-done.16.refs_6_), channel_id=1, source_target_pairs={{1,0},{2,1},{3,2},{4,3},{5,4},{6,5},{7,6},{0,7},{9,8},{10,9},{11,1... | collective-permute-start | bytes 393224 | tf_op jit(solution)/shard_map/ppermute | solution.py:233
  249.1 3.5 %collective-permute-done.13.refs_3_ = bf16[16,4096]{1,0:T(8,128)(2,1)S(1)} collective-permute-done((bf16[16,4096]{1,0:T(8,128)(2,1)S(1)}, bf16[16,4096]{1,0:T(8,128)(2,1)S(1)}, u32[]{:S(2)}, u32[]{:S(2)}) %collective-permute-start.13) | collective-permute-done | bytes 131104 | tf_op jit(solution)/shard_map/ppermute | solution.py:231
  252.6 6.2 %collective-permute-done.14.refs_4_ = bf16[16,4096]{1,0:T(8,128)(2,1)S(1)} collective-permute-done((bf16[16,4096]{1,0:T(8,128)(2,1)S(1)}, bf16[16,4096]{1,0:T(8,128)(2,1)S(1)}, u32[]{:S(2)}, u32[]{:S(2)}) %collective-permute-start.14) | collective-permute-done | bytes 131104 | tf_op jit(solution)/shard_map/ppermute | solution.py:231
  258.8 2.2 late_blocks.1
  261.0 4.6 %all-to-all-start.5 = ((bf16[16,128,512]{2,1,0:T(8,128)(2,1)}), bf16[16,128,512]{2,1,0:T(8,128)(2,1)}, u32[]{:S(2)}, u32[]{:S(2)}) async-start(bf16[16,128,512]{2,1,0:T(8,128)(2,1)} %late_blocks.1), calls=%async_computation.5 | async-start | bytes 4194304 | tf_op jit(solution)/shard_map/all_to_all | solution.py:251
  267.0 27.2 %all-to-all-done.5 = bf16[16,128,512]{2,1,0:T(8,128)(2,1)} async-done(((bf16[16,128,512]{2,1,0:T(8,128)(2,1)}), bf16[16,128,512]{2,1,0:T(8,128)(2,1)}, u32[]{:S(2)}, u32[]{:S(2)}) %all-to-all-start.5) | async-done | bytes 2097184 | tf_op jit(solution)/shard_map/all_to_all | solution.py:251
  294.1 1.2 copy-done.3
  295.4 1.0 copy-done.4
  296.4 1.0 copy-done.5
  297.5 5.7 %owner_step.1 = (f32[512,512]{1,0:T(8,128)}, f32[512,512]{1,0:T(8,128)}, bf16[512,512]{1,0:T(8,128)(2,1)}, bf16[512,512]{1,0:T(8,128)(2,1)}, bf16[512,512]{1,0:T(8,128)(2,1)}) custom-call(s32[2]{0:T(128)S(1)} %pad_add_fusion.info_ref, bf16[2048,512]{1,0:T(8,128)(2,1)S(1)} %bitcast.73, bf16[2048,512]{1,0:T(8,128)(2,1)} %bitcast.23.late_ref, ...), custom_call_target="tpu_custom_call" | custom-call | tf_op jit(solution)/shard_map/owner_step/pallas_call | solution.py:139
  (72 shorter events, 5.0 us)
Async XLA Ops:
  7.2 2.3 copy-start.6
  7.2 3.2 %copy-start.11 = (f32[1,4096]{1,0:T(1,128)S(1)}, f32[1,4096]{1,0:T(1,128)}, u32[]{:S(2)}) copy-start(f32[1,4096]{1,0:T(1,128)} %param.14) | copy-start | bytes 49156
  7.2 3.9 %copy-start = (bf16[2,64,4096]{2,1,0:T(8,128)(2,1)S(1)}, bf16[2,64,4096]{2,1,0:T(8,128)(2,1)}, u32[]{:S(2)}) copy-start(bf16[2,64,4096]{2,1,0:T(8,128)(2,1)} %param.13) | copy-start | bytes 3145732
  7.2 87.4 %all-gather.3.cloned.1.call-start = ((), (), s32[]{:S(2)}) async-start(), calls=%async_computation.6 | async-start | bytes 8912896 | tf_op jit(solution)/shard_map/all_gather | solution.py:184
  37.8 3.3 %collective-permute-start.1 = (bf16[8,128,512]{2,1,0:T(8,128)(2,1)}, bf16[8,128,512]{2,1,0:T(8,128)(2,1)}, u32[]{:S(2)}, u32[]{:S(2)}) collective-permute-start(bf16[8,128,512]{2,1,0:T(8,128)(2,1)} %all_to_all.30), channel_id=1, source_target_pairs={{0,8},{8,0},{16,24},{24,16},{32,40},{40,32},{48,56},{56,48},{64,72... | collective-permute-start | bytes 3145736 | tf_op jit(solution)/shard_map/ppermute | solution.py:202
  37.8 3.1 %collective-permute-start = (bf16[256,512]{1,0:T(8,128)(2,1)S(1)}, bf16[256,512]{1,0:T(8,128)(2,1)S(1)}, u32[]{:S(2)}, u32[]{:S(2)}) collective-permute-start(bf16[256,512]{1,0:T(8,128)(2,1)S(1)} %broadcast_select_fusion.5), channel_id=1, source_target_pairs={{0,8},{8,0},{16,24},{24,16},{32,40},{40,32},{48,56},{56,48},{64,72... | collective-permute-start | bytes 786440 | tf_op jit(solution)/shard_map/ppermute | solution.py:193
  93.1 0.7 copy-start.7
  93.1 0.8 copy-start.9
  101.8 8.6 %copy-start.13 = (s32[2,16,8]{1,2,0:T(8,128)S(1)}, s32[2,16,8]{1,2,0:T(8,128)}, u32[]{:S(2)}) copy-start(s32[2,16,8]{1,2,0:T(8,128)} %param.21) | copy-start | bytes 3076
  101.9 8.6 %copy-start.14 = (s32[2,16,8]{1,2,0:T(8,128)S(1)}, s32[2,16,8]{1,2,0:T(8,128)}, u32[]{:S(2)}) copy-start(s32[2,16,8]{1,2,0:T(8,128)} %param.22) | copy-start | bytes 3076
  101.9 37.8 %all-to-all-start.2 = ((bf16[8,16,4096]{2,1,0:T(8,128)(2,1)}), bf16[8,16,4096]{2,1,0:T(8,128)(2,1)S(1)}, u32[]{:S(2)}, u32[]{:S(2)}) async-start(bf16[8,16,4096]{2,1,0:T(8,128)(2,1)} %bitcast.19), calls=%async_computation.2 | async-start | bytes 2097152 | tf_op jit(solution)/shard_map/all_to_all | solution.py:220
  139.8 7.1 %collective-permute-start.2 = (bf16[16,4096]{1,0:T(8,128)(2,1)S(1)}, bf16[16,4096]{1,0:T(8,128)(2,1)S(1)}, u32[]{:S(2)}, u32[]{:S(2)}) collective-permute-start(bf16[16,4096]{1,0:T(8,128)(2,1)S(1)} %add_convert_fusion), channel_id=1, source_target_pairs={{0,128},{1,129},{2,130},{3,131},{4,132},{5,133},{6,134},{7,135},{8... | collective-permute-start | bytes 393224 | tf_op jit(solution)/shard_map/ppermute | solution.py:263
  147.0 33.5 %all-to-all-start.3 = ((bf16[16,128,512]{2,1,0:T(8,128)(2,1)}), bf16[16,128,512]{2,1,0:T(8,128)(2,1)S(1)}, u32[]{:S(2)}, u32[]{:S(2)}) async-start(bf16[16,128,512]{2,1,0:T(8,128)(2,1)} %early_blocks.1), calls=%async_computation.3 | async-start | bytes 4194304 | tf_op jit(solution)/shard_map/all_to_all | solution.py:251
  152.3 6.8 %collective-permute-start.3 = (bf16[16,4096]{1,0:T(8,128)(2,1)S(1)}, bf16[16,4096]{1,0:T(8,128)(2,1)S(1)}, u32[]{:S(2)}, u32[]{:S(2)}) collective-permute-start(bf16[16,4096]{1,0:T(8,128)(2,1)S(1)} %fusion.19.refs_0_), channel_id=1, source_target_pairs={{0,1},{1,2},{2,3},{3,4},{4,5},{5,6},{6,7},{7,0},{8,9},{9,10},{10,1... | collective-permute-start | bytes 393224 | tf_op jit(solution)/shard_map/ppermute | solution.py:231
  152.5 6.7 %collective-permute-start.7 = (bf16[16,4096]{1,0:T(8,128)(2,1)S(1)}, bf16[16,4096]{1,0:T(8,128)(2,1)S(1)}, u32[]{:S(2)}, u32[]{:S(2)}) collective-permute-start(bf16[16,4096]{1,0:T(8,128)(2,1)S(1)} %fusion.19.refs_0_), channel_id=1, source_target_pairs={{1,0},{2,1},{3,2},{4,3},{5,4},{6,5},{7,6},{0,7},{9,8},{10,9},{11,1... | collective-permute-start | bytes 393224 | tf_op jit(solution)/shard_map/ppermute | solution.py:233
  159.1 6.2 %collective-permute-start.4 = (bf16[16,4096]{1,0:T(8,128)(2,1)S(1)}, bf16[16,4096]{1,0:T(8,128)(2,1)S(1)}, u32[]{:S(2)}, u32[]{:S(2)}) collective-permute-start(bf16[16,4096]{1,0:T(8,128)(2,1)S(1)} %collective-permute-done.3.refs_1_), channel_id=1, source_target_pairs={{0,1},{1,2},{2,3},{3,4},{4,5},{5,6},{6,7},{7,0},{8,9},{9,10},{10,1... | collective-permute-start | bytes 393224 | tf_op jit(solution)/shard_map/ppermute | solution.py:231
  159.1 6.2 %collective-permute-start.8 = (bf16[16,4096]{1,0:T(8,128)(2,1)S(1)}, bf16[16,4096]{1,0:T(8,128)(2,1)S(1)}, u32[]{:S(2)}, u32[]{:S(2)}) collective-permute-start(bf16[16,4096]{1,0:T(8,128)(2,1)S(1)} %collective-permute-done.7.refs_7_), channel_id=1, source_target_pairs={{1,0},{2,1},{3,2},{4,3},{5,4},{6,5},{7,6},{0,7},{9,8},{10,9},{11,1... | collective-permute-start | bytes 393224 | tf_op jit(solution)/shard_map/ppermute | solution.py:233
  165.3 6.2 %collective-permute-start.5 = (bf16[16,4096]{1,0:T(8,128)(2,1)S(1)}, bf16[16,4096]{1,0:T(8,128)(2,1)S(1)}, u32[]{:S(2)}, u32[]{:S(2)}) collective-permute-start(bf16[16,4096]{1,0:T(8,128)(2,1)S(1)} %collective-permute-done.4.refs_2_), channel_id=1, source_target_pairs={{0,1},{1,2},{2,3},{3,4},{4,5},{5,6},{6,7},{7,0},{8,9},{9,10},{10,1... | collective-permute-start | bytes 393224 | tf_op jit(solution)/shard_map/ppermute | solution.py:231
  165.3 6.2 %collective-permute-start.9 = (bf16[16,4096]{1,0:T(8,128)(2,1)S(1)}, bf16[16,4096]{1,0:T(8,128)(2,1)S(1)}, u32[]{:S(2)}, u32[]{:S(2)}) collective-permute-start(bf16[16,4096]{1,0:T(8,128)(2,1)S(1)} %collective-permute-done.8.refs_6_), channel_id=1, source_target_pairs={{1,0},{2,1},{3,2},{4,3},{5,4},{6,5},{7,6},{0,7},{9,8},{10,9},{11,1... | collective-permute-start | bytes 393224 | tf_op jit(solution)/shard_map/ppermute | solution.py:233
  171.5 6.2 %collective-permute-start.6 = (bf16[16,4096]{1,0:T(8,128)(2,1)S(1)}, bf16[16,4096]{1,0:T(8,128)(2,1)S(1)}, u32[]{:S(2)}, u32[]{:S(2)}) collective-permute-start(bf16[16,4096]{1,0:T(8,128)(2,1)S(1)} %collective-permute-done.5.refs_3_), channel_id=1, source_target_pairs={{0,1},{1,2},{2,3},{3,4},{4,5},{5,6},{6,7},{7,0},{8,9},{9,10},{10,1... | collective-permute-start | bytes 393224 | tf_op jit(solution)/shard_map/ppermute | solution.py:231
  178.3 1.0 copy-start.1
  179.3 6.3 %copy-start.8 = (f32[128,512]{1,0:T(8,128)S(1)}, f32[128,512]{1,0:T(8,128)}, u32[]{:S(2)}) copy-start(f32[128,512]{1,0:T(8,128)} %copy-done.7) | copy-start | bytes 786436
  180.5 5.1 %copy-start.10 = (f32[128,512]{1,0:T(8,128)S(1)}, f32[128,512]{1,0:T(8,128)}, u32[]{:S(2)}) copy-start(f32[128,512]{1,0:T(8,128)} %copy-done.9) | copy-start | bytes 786436
  191.8 31.4 %copy-start.12 = (f32[1,4096]{1,0:T(1,128)S(1)}, f32[1,4096]{1,0:T(1,128)}, u32[]{:S(2)}) copy-start(f32[1,4096]{1,0:T(1,128)} %param.14) | copy-start | bytes 49156
  223.5 8.4 %collective-permute-start.10 = (bf16[16,4096]{1,0:T(8,128)(2,1)S(1)}, bf16[16,4096]{1,0:T(8,128)(2,1)S(1)}, u32[]{:S(2)}, u32[]{:S(2)}) collective-permute-start(bf16[16,4096]{1,0:T(8,128)(2,1)S(1)} %fusion.16), channel_id=1, source_target_pairs={{128,0},{129,1},{130,2},{131,3},{132,4},{133,5},{134,6},{135,7},{1... | collective-permute-start | bytes 393224 | tf_op jit(solution)/shard_map/ppermute | solution.py:278
  231.9 6.4 %collective-permute-start.11 = (bf16[16,4096]{1,0:T(8,128)(2,1)S(1)}, bf16[16,4096]{1,0:T(8,128)(2,1)S(1)}, u32[]{:S(2)}, u32[]{:S(2)}) collective-permute-start(bf16[16,4096]{1,0:T(8,128)(2,1)S(1)} %collective-permute-done.10.refs_0_), channel_id=1, source_target_pairs={{0,1},{1,2},{2,3},{3,4},{4,5},{5,6},{6,7},{7,0},{8,9},{9,10},{10,1... | collective-permute-start | bytes 393224 | tf_op jit(solution)/shard_map/ppermute | solution.py:231
  232.4 5.9 %collective-permute-start.15 = (bf16[16,4096]{1,0:T(8,128)(2,1)S(1)}, bf16[16,4096]{1,0:T(8,128)(2,1)S(1)}, u32[]{:S(2)}, u32[]{:S(2)}) collective-permute-start(bf16[16,4096]{1,0:T(8,128)(2,1)S(1)} %collective-permute-done.10.refs_0_), channel_id=1, source_target_pairs={{1,0},{2,1},{3,2},{4,3},{5,4},{6,5},{7,6},{0,7},{9,8},{10,9},{11,1... | collective-permute-start | bytes 393224 | tf_op jit(solution)/shard_map/ppermute | solution.py:233
  238.3 7.6 %collective-permute-start.12 = (bf16[16,4096]{1,0:T(8,128)(2,1)S(1)}, bf16[16,4096]{1,0:T(8,128)(2,1)S(1)}, u32[]{:S(2)}, u32[]{:S(2)}) collective-permute-start(bf16[16,4096]{1,0:T(8,128)(2,1)S(1)} %collective-permute-done.11.refs_1_), channel_id=1, source_target_pairs={{0,1},{1,2},{2,3},{3,4},{4,5},{5,6},{6,7},{7,0},{8,9},{9,10},{10,1... | collective-permute-start | bytes 393224 | tf_op jit(solution)/shard_map/ppermute | solution.py:231
  238.3 7.6 %collective-permute-start.16 = (bf16[16,4096]{1,0:T(8,128)(2,1)S(1)}, bf16[16,4096]{1,0:T(8,128)(2,1)S(1)}, u32[]{:S(2)}, u32[]{:S(2)}) collective-permute-start(bf16[16,4096]{1,0:T(8,128)(2,1)S(1)} %collective-permute-done.15.refs_7_), channel_id=1, source_target_pairs={{1,0},{2,1},{3,2},{4,3},{5,4},{6,5},{7,6},{0,7},{9,8},{10,9},{11,1... | collective-permute-start | bytes 393224 | tf_op jit(solution)/shard_map/ppermute | solution.py:233
  245.9 6.7 %collective-permute-start.13 = (bf16[16,4096]{1,0:T(8,128)(2,1)S(1)}, bf16[16,4096]{1,0:T(8,128)(2,1)S(1)}, u32[]{:S(2)}, u32[]{:S(2)}) collective-permute-start(bf16[16,4096]{1,0:T(8,128)(2,1)S(1)} %collective-permute-done.12.refs_2_), channel_id=1, source_target_pairs={{0,1},{1,2},{2,3},{3,4},{4,5},{5,6},{6,7},{7,0},{8,9},{9,10},{10,1... | collective-permute-start | bytes 393224 | tf_op jit(solution)/shard_map/ppermute | solution.py:231
  245.9 6.7 %collective-permute-start.17 = (bf16[16,4096]{1,0:T(8,128)(2,1)S(1)}, bf16[16,4096]{1,0:T(8,128)(2,1)S(1)}, u32[]{:S(2)}, u32[]{:S(2)}) collective-permute-start(bf16[16,4096]{1,0:T(8,128)(2,1)S(1)} %collective-permute-done.16.refs_6_), channel_id=1, source_target_pairs={{1,0},{2,1},{3,2},{4,3},{5,4},{6,5},{7,6},{0,7},{9,8},{10,9},{11,1... | collective-permute-start | bytes 393224 | tf_op jit(solution)/shard_map/ppermute | solution.py:233
  252.6 6.2 %collective-permute-start.14 = (bf16[16,4096]{1,0:T(8,128)(2,1)S(1)}, bf16[16,4096]{1,0:T(8,128)(2,1)S(1)}, u32[]{:S(2)}, u32[]{:S(2)}) collective-permute-start(bf16[16,4096]{1,0:T(8,128)(2,1)S(1)} %collective-permute-done.13.refs_3_), channel_id=1, source_target_pairs={{0,1},{1,2},{2,3},{3,4},{4,5},{5,6},{6,7},{7,0},{8,9},{9,10},{10,1... | collective-permute-start | bytes 393224 | tf_op jit(solution)/shard_map/ppermute | solution.py:231
  261.0 33.2 %copy-start.2 = (f32[1,1,512,512]{3,2,1,0:T(8,128)S(1)}, f32[1,1,512,512]{3,2,1,0:T(8,128)}, u32[]{:S(2)}) copy-start(f32[1,1,512,512]{3,2,1,0:T(8,128)} %param.17) | copy-start | bytes 3145732
  261.0 33.2 %all-to-all-start.5 = ((bf16[16,128,512]{2,1,0:T(8,128)(2,1)}), bf16[16,128,512]{2,1,0:T(8,128)(2,1)}, u32[]{:S(2)}, u32[]{:S(2)}) async-start(bf16[16,128,512]{2,1,0:T(8,128)(2,1)} %late_blocks.1), calls=%async_computation.5 | async-start | bytes 4194304 | tf_op jit(solution)/shard_map/all_to_all | solution.py:251
  294.1 1.2 copy-start.3
  295.4 1.0 copy-start.4
  296.4 1.0 copy-start.5
Sparse Core Ops, SparseCore 0:
  10.5 84.1 all-gather.2
